TPU v7x, 1024 devices: a whole 4x8x16 slice. The times are simulated.
1024 devices in a mesh: island: 16 (over y, core), ep: 16 (over z), tp: 4 (over x).
Axes of the slice: x: 4, y: 8, z: 16, core: 2. Of those that a mesh axis runs over, the one named last changes fastest.
Arguments:
- tokens: bfloat16 [32768, 2048], P(('island', 'ep')), may hold values from -6 to 6
- cotangent: bfloat16 [32768, 2048], P(('island', 'ep')), may hold values from -6 to 6
- expert_ids: int32 [32768, 1], P(('island', 'ep')), may hold values from 0 to 15; in each aligned block of 128 rows (0 to 127, 128 to 255, ...) at most 10 rows name the same one
- gate_probs: float32 [32768, 1], P(('island', 'ep')), may hold values from 0.1 to 1
- w_gate: bfloat16 [16, 2048, 768], P('ep', None, 'tp'), may hold values from -0.125 to 0.125
- w_up: bfloat16 [16, 2048, 768], P('ep', None, 'tp'), may hold values from -0.125 to 0.125
- w_down: bfloat16 [16, 768, 2048], P('ep', 'tp'), may hold values from -0.21875 to 0.21875
Outputs:
- token_grad: bfloat16 [32768, 2048], P(('island', 'ep'), 'tp')
- prob_grad: float32 [32768, 1], P(('island', 'ep'))
- grad_gate: float32 [16, 2048, 768], P('ep', 'island', 'tp')
- grad_up: float32 [16, 2048, 768], P('ep', 'island', 'tp')
- grad_down: float32 [16, 768, 2048], P('ep', 'tp', 'island')
Inputs may be any that keep to these rules, and one draw needn't show every extreme that they name: `expert_ids`: each row names one expert; in each aligned block of 128 rows (one index of island and ep) no expert is named by more than 10 rows, a bound that some block reaches.
All inputs are finite; a program needn't handle non-finite values.
Results may differ from a plain program's by a relative error of at most 0.025.
Values may be sent and summed in bfloat16 or wider, within the bound.
A program may use at most 32 MiB of HBM per device.

v0:
```python
import jax
import jax.numpy as jnp
from jax import lax
from jax.sharding import PartitionSpec as P


def shards(tokens, cotangent, expert_ids, gate_probs, w_gate, w_up, w_down):
    tok_rows, width = tokens.shape
    top_count = expert_ids.shape[1]
    local_experts = w_gate.shape[0]
    expert_total = local_experts * lax.axis_size("ep")
    capacity = min(tok_rows, 5 * tok_rows * top_count // (4 * expert_total))
    flat_ids = expert_ids.reshape(-1)
    onehot = (flat_ids[:, None] == jnp.arange(expert_total, dtype=jnp.int32)[None, :]).astype(
        jnp.int32
    )
    ranks = jnp.sum((jnp.cumsum(onehot, 0) - onehot) * onehot, 1)
    dest = flat_ids * capacity + ranks
    owners = jnp.arange(tok_rows * top_count, dtype=jnp.int32) // top_count
    source = jnp.full((expert_total * capacity,), tok_rows, jnp.int32).at[dest].set(owners)
    weights = (
        jnp.zeros((expert_total * capacity,), jnp.float32).at[dest].set(gate_probs.reshape(-1))
    )
    zero_row = jnp.zeros((1, width), jnp.bfloat16)
    send_x = jnp.concatenate([tokens, zero_row], 0)[source].reshape(expert_total, capacity, width)
    send_dy = jnp.concatenate([cotangent, zero_row], 0)[source].reshape(
        expert_total, capacity, width
    )
    send_p = weights.reshape(expert_total, capacity)
    recv_x, recv_dy, recv_p = (
        lax.all_to_all(send_x, "ep", split_axis=0, concat_axis=1, tiled=True),
        lax.all_to_all(send_dy, "ep", split_axis=0, concat_axis=1, tiled=True),
        lax.all_to_all(
            send_p.astype(jnp.bfloat16), "ep", split_axis=0, concat_axis=1, tiled=True
        ).astype(send_p.dtype),
    )
    gate = jnp.einsum("emd,edf->emf", recv_x, w_gate, preferred_element_type=jnp.float32)
    up = jnp.einsum("emd,edf->emf", recv_x, w_up, preferred_element_type=jnp.float32)
    sigma = jax.nn.sigmoid(gate)
    active = gate * sigma
    hidden = (active * up).astype(jnp.bfloat16)
    back = jnp.einsum("emd,efd->emf", recv_dy, w_down, preferred_element_type=jnp.float32)
    prob_part = jnp.sum(hidden.astype(jnp.float32) * back, 2)
    scale = recv_p[:, :, None]
    d_hidden = back * scale
    d_gate = (d_hidden * up * sigma * (1.0 + gate * (1.0 - sigma))).astype(jnp.bfloat16)
    d_up = (d_hidden * active).astype(jnp.bfloat16)
    scaled_hidden = (hidden.astype(jnp.float32) * scale).astype(jnp.bfloat16)
    down_local = jnp.einsum(
        "emd,emf->edf", recv_dy, scaled_hidden, preferred_element_type=jnp.float32
    )
    gate_local = jnp.einsum("emd,emf->edf", recv_x, d_gate, preferred_element_type=jnp.float32)
    up_local = jnp.einsum("emd,emf->edf", recv_x, d_up, preferred_element_type=jnp.float32)
    grad_gate, grad_up, down_total = (
        lax.psum_scatter(
            gate_local.astype(jnp.bfloat16), "island", scatter_dimension=1, tiled=True
        ).astype(jnp.float32),
        lax.psum_scatter(
            up_local.astype(jnp.bfloat16), "island", scatter_dimension=1, tiled=True
        ).astype(jnp.float32),
        lax.psum_scatter(
            down_local.astype(jnp.bfloat16), "island", scatter_dimension=1, tiled=True
        ).astype(jnp.float32),
    )
    grad_down = jnp.transpose(down_total, (0, 2, 1))
    input_part = jnp.einsum("emf,edf->emd", d_gate, w_gate, preferred_element_type=jnp.float32)
    input_part = input_part + jnp.einsum(
        "emf,edf->emd", d_up, w_up, preferred_element_type=jnp.float32
    )
    row_grad = lax.psum_scatter(
        input_part.astype(jnp.bfloat16), "tp", scatter_dimension=2, tiled=True
    )
    prob_rows = lax.psum(prob_part, "tp")
    back_rows, back_probs = (
        lax.all_to_all(row_grad, "ep", split_axis=1, concat_axis=0, tiled=True),
        lax.all_to_all(
            prob_rows.astype(jnp.bfloat16), "ep", split_axis=1, concat_axis=0, tiled=True
        ).astype(prob_rows.dtype),
    )
    quarter_width = back_rows.shape[2]
    back_flat = back_rows.reshape(expert_total * capacity, quarter_width)
    pair_rows = back_flat[dest].astype(jnp.float32).reshape(tok_rows, top_count, quarter_width)
    token_grad = jnp.sum(pair_rows, 1).astype(jnp.bfloat16)
    prob_grad = back_probs.reshape(-1)[dest].reshape(tok_rows, top_count)
    return (token_grad, prob_grad, grad_gate, grad_up, grad_down)


def solution(mesh):
    in_specs = (
        P(("island", "ep"), None),
        P(("island", "ep"), None),
        P(("island", "ep"), None),
        P(("island", "ep"), None),
        P("ep", None, "tp"),
        P("ep", None, "tp"),
        P("ep", "tp", None),
    )
    out_specs = (
        P(("island", "ep"), "tp"),
        P(("island", "ep"), None),
        P("ep", "island", "tp"),
        P("ep", "island", "tp"),
        P("ep", "tp", "island"),
    )
    return jax.shard_map(shards, mesh=mesh, in_specs=in_specs, out_specs=out_specs, check_vma=False)
```

profile of v0, /device:TPU:1, one launch (start us, length us, event | category | flops | bytes accessed | tf_op | source)
XLA Modules:
  0.0 403.2 jit_solution(13806463669463048723)
XLA Ops:
  11.5 19.4 %all-to-all-start.1 = ((bf16[16,1,10]{2,1,0:T(2,128)(2,1)}), bf16[16,1,10]{2,1,0:T(2,128)(2,1)S(1)}, u32[]{:S(2)}, u32[]{:S(2)}) async-start(bf16[16,1,10]{2,1,0:T(2,128)(2,1)} %convert_element_type.119), calls=%async_computation.1 | async-start | bytes 16384 | tf_op jit(solution)/shard_map/all_to_all | solution.py:33
  35.3 6.9 %all-to-all-done.1 = bf16[16,1,10]{2,1,0:T(2,128)(2,1)S(1)} async-done(((bf16[16,1,10]{2,1,0:T(2,128)(2,1)}), bf16[16,1,10]{2,1,0:T(2,128)(2,1)S(1)}, u32[]{:S(2)}, u32[]{:S(2)}) %all-to-all-start.1) | async-done | bytes 352 | tf_op jit(solution)/shard_map/all_to_all | solution.py:33
  42.1 4.6 %all-to-all-start.2 = ((bf16[16,10,2048]{2,1,0:T(8,128)(2,1)}), bf16[16,10,2048]{2,1,0:T(8,128)(2,1)S(1)}, u32[]{:S(2)}, u32[]{:S(2)}) async-start(bf16[16,10,2048]{2,1,0:T(8,128)(2,1)} %reshape.156), calls=%async_computation.2 | async-start | bytes 2097152 | tf_op jit(solution)/shard_map/all_to_all | solution.py:31
  49.1 42.0 %all-to-all-done.2 = bf16[16,10,2048]{2,1,0:T(8,128)(2,1)S(1)} async-done(((bf16[16,10,2048]{2,1,0:T(8,128)(2,1)}), bf16[16,10,2048]{2,1,0:T(8,128)(2,1)S(1)}, u32[]{:S(2)}, u32[]{:S(2)}) %all-to-all-start.2) | async-done | bytes 655392 | tf_op jit(solution)/shard_map/all_to_all | solution.py:31
  91.1 13.7 %all-to-all-start = ((bf16[16,10,2048]{2,1,0:T(8,128)(2,1)}), bf16[16,10,2048]{2,1,0:T(8,128)(2,1)S(1)}, u32[]{:S(2)}, u32[]{:S(2)}) async-start(bf16[16,10,2048]{2,1,0:T(8,128)(2,1)} %reshape.152), calls=%async_computation | async-start | bytes 2097152 | tf_op jit(solution)/shard_map/all_to_all | solution.py:32
  105.2 1.5 fusion.10
  107.2 42.8 %all-to-all-done = bf16[16,10,2048]{2,1,0:T(8,128)(2,1)S(1)} async-done(((bf16[16,10,2048]{2,1,0:T(8,128)(2,1)}), bf16[16,10,2048]{2,1,0:T(8,128)(2,1)S(1)}, u32[]{:S(2)}, u32[]{:S(2)}) %all-to-all-start) | async-done | bytes 655392 | tf_op jit(solution)/shard_map/all_to_all | solution.py:32
  150.2 1.7 fusion.14
  154.3 1.4 fusion.3
  155.7 4.5 %copy.21 = bf16[1,2048,192]{2,0,1:T(2,128)(2,1)S(1)} copy(bf16[1,2048,192]{1,2,0:T(8,128)(2,1)} %fusion.3) | data formatting | bytes 1572864
  161.5 2.2 fusion.1
  163.7 4.5 %copy.17 = bf16[1,2048,192]{2,0,1:T(2,128)(2,1)S(1)} copy(bf16[1,2048,192]{1,2,0:T(8,128)(2,1)} %fusion.1) | data formatting | bytes 1572864
  169.6 2.2 fusion.2
  171.8 4.6 %copy.19 = bf16[1,2048,192]{2,0,1:T(2,128)(2,1)S(1)} copy(bf16[1,2048,192]{1,2,0:T(8,128)(2,1)} %fusion.2) | data formatting | bytes 1572864
  177.5 9.4 %psum.7 = bf16[1,160]{1,0:T(2,128)(2,1)S(1)} all-reduce(f32[1,160]{1,0:T(1,128)S(1)} %bitcast.84), channel_id=1, replica_groups=mesh['island'=16,'ep'=16,'tp'=4] {'tp'}, use_global_device_ids=true, to_apply=%region_6.7 | all-reduce | flops 160 | bytes 960 | tf_op jit(solution)/shard_map/psum | solution.py:73
  187.6 12.9 %all-to-all-start.4 = ((bf16[1,16,10]{2,0,1:T(2,128)(2,1)}), bf16[1,16,10]{2,0,1:T(2,128)(2,1)S(1)}, u32[]{:S(2)}, u32[]{:S(2)}) async-start(bf16[1,16,10]{2,0,1:T(2,128)(2,1)} %all_to_all.20), calls=%async_computation.5 | async-start | bytes 16384 | tf_op jit(solution)/shard_map/all_to_all | solution.py:76
  202.2 1.6 reduce.12
  204.6 7.1 %all-to-all-done.4 = bf16[1,16,10]{2,0,1:T(2,128)(2,1)S(1)} async-done(((bf16[1,16,10]{2,0,1:T(2,128)(2,1)}), bf16[1,16,10]{2,0,1:T(2,128)(2,1)S(1)}, u32[]{:S(2)}, u32[]{:S(2)}) %all-to-all-start.4) | async-done | bytes 352 | tf_op jit(solution)/shard_map/all_to_all | solution.py:76
  211.7 4.3 %all-to-all-start.3 = ((bf16[16,2,2560]{2,1,0:T(2,128)(2,1)}), bf16[16,2,2560]{2,1,0:T(2,128)(2,1)S(1)}, u32[]{:S(2)}, u32[]{:S(2)}) async-start(bf16[16,2,2560]{2,1,0:T(2,128)(2,1)} %reshape.240), calls=%async_computation.4 | async-start | bytes 327680 | tf_op jit(solution)/shard_map/all_to_all | solution.py:75
  216.2 1.8 gather_fusion.3
  217.9 39.5 %reduce-scatter.17.cloned.1.call-done = bf16[128,192]{1,0:T(8,128)(2,1)} async-done(((bf16[2048,192]{1,0:T(8,128)(2,1)}), bf16[128,192]{1,0:T(8,128)(2,1)}) %reduce-scatter.17.cloned.1.call-update) | async-done | bytes 49168
  258.4 66.8 %reduce-scatter.13.cloned.1.call-done = bf16[128,192]{1,0:T(8,128)(2,1)} async-done(((bf16[2048,192]{1,0:T(8,128)(2,1)}), bf16[128,192]{1,0:T(8,128)(2,1)}) %reduce-scatter.13.cloned.1.call-update) | async-done | bytes 49168
  327.0 65.7 %reduce-scatter.15.cloned.1.call-done = bf16[128,192]{1,0:T(8,128)(2,1)} async-done(((bf16[2048,192]{1,0:T(8,128)(2,1)}), bf16[128,192]{1,0:T(8,128)(2,1)}) %reduce-scatter.15.cloned.1.call-update) | async-done | bytes 49168
  395.2 1.5 gather_fusion.2
  (66 shorter events, 26.5 us)
Async XLA Ops:
  7.2 99.6 %copy-start = (bf16[1,2048,192]{1,2,0:T(8,128)(2,1)S(1)}, bf16[1,2048,192]{1,2,0:T(8,128)(2,1)}, u32[]{:S(2)}) copy-start(bf16[1,2048,192]{1,2,0:T(8,128)(2,1)} %param.11) | copy-start | bytes 2359300
  11.5 30.6 %all-to-all-start.1 = ((bf16[16,1,10]{2,1,0:T(2,128)(2,1)}), bf16[16,1,10]{2,1,0:T(2,128)(2,1)S(1)}, u32[]{:S(2)}, u32[]{:S(2)}) async-start(bf16[16,1,10]{2,1,0:T(2,128)(2,1)} %convert_element_type.119), calls=%async_computation.1 | async-start | bytes 16384 | tf_op jit(solution)/shard_map/all_to_all | solution.py:33
  34.1 12.7 %copy-start.2 = (bf16[128,2048]{1,0:T(8,128)(2,1)S(1)}, bf16[128,2048]{1,0:T(8,128)(2,1)}, u32[]{:S(2)}) copy-start(bf16[128,2048]{1,0:T(8,128)(2,1)} %param.8) | copy-start | bytes 1572868
  42.1 48.9 %all-to-all-start.2 = ((bf16[16,10,2048]{2,1,0:T(8,128)(2,1)}), bf16[16,10,2048]{2,1,0:T(8,128)(2,1)S(1)}, u32[]{:S(2)}, u32[]{:S(2)}) async-start(bf16[16,10,2048]{2,1,0:T(8,128)(2,1)} %reshape.156), calls=%async_computation.2 | async-start | bytes 2097152 | tf_op jit(solution)/shard_map/all_to_all | solution.py:31
  91.1 58.9 %all-to-all-start = ((bf16[16,10,2048]{2,1,0:T(8,128)(2,1)}), bf16[16,10,2048]{2,1,0:T(8,128)(2,1)S(1)}, u32[]{:S(2)}, u32[]{:S(2)}) async-start(bf16[16,10,2048]{2,1,0:T(8,128)(2,1)} %reshape.152), calls=%async_computation | async-start | bytes 2097152 | tf_op jit(solution)/shard_map/all_to_all | solution.py:32
  104.8 95.7 %reduce-scatter.11.cloned.1.call-start = ((), (), s32[]{:S(2)}) async-start(), calls=%async_computation.9 | async-start | bytes 819200 | tf_op jit(solution)/shard_map/reduce_scatter | solution.py:70
  151.9 0.6 copy-start.4
  151.9 1.0 copy-start.3
  151.9 1.2 copy-start.1
  154.3 103.1 %reduce-scatter.17.cloned.1.call-start = ((), (), s32[]{:S(2)}) async-start(), calls=%async_computation.12 | async-start | bytes 1114112
  161.4 163.8 %reduce-scatter.13.cloned.1.call-start = ((), (), s32[]{:S(2)}) async-start(), calls=%async_computation.10 | async-start | bytes 1114112
  169.5 223.2 %reduce-scatter.15.cloned.1.call-start = ((), (), s32[]{:S(2)}) async-start(), calls=%async_computation.11 | async-start | bytes 1114112
  187.6 24.1 %all-to-all-start.4 = ((bf16[1,16,10]{2,0,1:T(2,128)(2,1)}), bf16[1,16,10]{2,0,1:T(2,128)(2,1)S(1)}, u32[]{:S(2)}, u32[]{:S(2)}) async-start(bf16[1,16,10]{2,0,1:T(2,128)(2,1)} %all_to_all.20), calls=%async_computation.5 | async-start | bytes 16384 | tf_op jit(solution)/shard_map/all_to_all | solution.py:76
  211.7 183.3 %all-to-all-start.3 = ((bf16[16,2,2560]{2,1,0:T(2,128)(2,1)}), bf16[16,2,2560]{2,1,0:T(2,128)(2,1)S(1)}, u32[]{:S(2)}, u32[]{:S(2)}) async-start(bf16[16,2,2560]{2,1,0:T(2,128)(2,1)} %reshape.240), calls=%async_computation.4 | async-start | bytes 327680 | tf_op jit(solution)/shard_map/all_to_all | solution.py:75
Sparse Core Ops, SparseCore 0:
  154.4 32.6 reduce-scatter.10
  190.5 66.8 reduce-scatter.16
  261.1 64.0 reduce-scatter.12
  328.5 64.1 reduce-scatter.14
where the time goes:
time: 405 us; the launch traced here: 403 us
  waiting for transfers between devices  271 us (67%)
  starting transfers between devices  55.1 us (14%)
  local copies, waits for them, and re-layouts  36.8 us (9%)
  between operations  14.1 us (3%)
  matrix products  10.9 us (3%)
  blocking collectives  9.36 us (2%)
  other arithmetic  6.12 us (2%)
    unnamed x7, waiting for transfers between devices  172 us
    all_to_all x1, waiting for transfers between devices, shards(): lax.all_to_all(send_dy, 'ep', split_axis=0, concat_axis=1, tiled=True)  42.8 us
    all_to_all x1, waiting for transfers between devices, shards(): lax.all_to_all(send_x, 'ep', split_axis=0, concat_axis=1, tiled=True)  42 us
    unnamed x26, local copies, waits for them, and re-layouts  22.6 us
    all_to_all x1, starting transfers between devices, shards(): lax.all_to_all(send_p.astype(jnp.bfloat16), 'ep', split_axis=0, concat_ax...  19.4 us
    all_to_all x1, starting transfers between devices, shards(): lax.all_to_all(send_dy, 'ep', split_axis=0, concat_axis=1, tiled=True)  13.7 us
    all_to_all x1, starting transfers between devices, shards(): lax.all_to_all(prob_rows.astype(jnp.bfloat16), 'ep', split_axis=1, concat...  12.9 us
    psum x1, blocking collectives, shards(): prob_rows = lax.psum(prob_part, 'tp')  9.36 us
  transfers between devices with their start and end apart: 9, of which 7 were waited for; matrix products, arithmetic and copies ran while one was open for 11% of the time, Pallas kernels for 0%

commit v1 on v0

v1 whole, which is shorter than its diff:
```python
import functools

import jax
import jax.numpy as jnp
from jax import lax
from jax.experimental import pallas as pl
from jax.experimental.pallas import tpu as pltpu
from jax.sharding import PartitionSpec as P

CAP = 10
ROWS = 16
SPARE = ROWS - CAP
LANES = 128
TAIL = 4 * LANES
BF = jnp.bfloat16
F32 = jnp.float32
MESH = pl.DeviceIdType.MESH
NT = ((1,), (1,))


def dot(a, b, dims=((1,), (0,)), precision=None):
    return lax.dot_general(
        a, b, (dims, ((), ())), preferred_element_type=F32, precision=precision
    )


def iota(shape, dim):
    return lax.broadcasted_iota(jnp.int32, shape, dim)


def hot(condition):
    return jnp.where(condition, 1.0, 0.0).astype(BF)


def kernel(
    nz, ny,
    tok, cot, ids_ref, probs_ref, wg, wu, wd,
    tg_ref, pg_ref, gg_ref, gu_ref, gd_ref,
    w, tq, cq, sb, rb, xs, ds, mx, md, gt, mgt, ch, cs, yl, yr, ip, xa, xl, xr, pk, rs, rr,
    ld, zs, zr, fs, fr, ms, mr, ps, pr, hs, hr, ys, yrs, vs, vr,
):
    t, z, island = lax.axis_index("tp"), lax.axis_index("ep"), lax.axis_index("island")
    y = lax.div(island, 2)
    core = island - 2 * y
    toks, quarter = tq.shape
    ff = wg.shape[0]
    m = nz * CAP
    n = nz * ROWS
    half = m // 2
    band = xs.shape[3]
    pairs = xs.shape[0]
    hz, hy = nz // 2, ny // 2
    fh = 3 * ff // 2
    part_a, part_b = pl.ds(0, fh), pl.ds(fh, fh)

    def tp_at(r):
        return {"tp": lax.rem(t + r, 4)}

    def ep_at(d):
        return {"ep": lax.rem(z + d, nz)}

    def y_at(d):
        return {"island": 2 * lax.rem(y + d, ny) + core}

    mate = {"island": 2 * y + 1 - core}

    def remote(src, dst, ssem, rsem, device):
        return pltpu.make_async_remote_copy(
            src_ref=src, dst_ref=dst, send_sem=ssem, recv_sem=rsem,
            device_id=device, device_id_type=MESH,
        )

    loads = [
        pltpu.make_async_copy(tok.at[:, pl.ds(pl.multiple_of(t * quarter, quarter), quarter)], tq, ld.at[0]),
        pltpu.make_async_copy(cot.at[:, pl.ds(pl.multiple_of(t * quarter, quarter), quarter)], cq, ld.at[1]),
        pltpu.make_async_copy(wg, w.at[pl.ds(0, ff)], ld.at[2]),
        pltpu.make_async_copy(wu, w.at[pl.ds(ff, ff)], ld.at[3]),
        pltpu.make_async_copy(wd, w.at[pl.ds(2 * ff, ff)], ld.at[4]),
    ]
    for copy in loads:
        copy.start()

    barrier = pltpu.get_barrier_semaphore()
    peers = [ep_at(d) for d in range(1, nz)] + [tp_at(r) for r in (1, 2, 3)]
    peers += [y_at(1), y_at(ny - 1), mate]
    for peer in peers:
        pl.semaphore_signal(barrier, inc=1, device_id=peer, device_id_type=MESH)

    ids = ids_ref[...]
    probs = probs_ref[...]
    named = hot(iota((nz, toks), 0) == ids)
    earlier = hot(iota((toks, toks), 0) < iota((toks, toks), 1))
    rank = jnp.sum(named.astype(F32) * dot(named, earlier), 0, keepdims=True)
    eye = iota((toks, toks), 0) == iota((toks, toks), 1)

    def column(row):
        return jnp.sum(jnp.where(eye, row, 0.0), 1, keepdims=True)

    probs_col = column(probs)
    ids_col = column(ids.astype(F32)).astype(jnp.int32)
    rank_col = column(rank).astype(jnp.int32)
    rank = rank.astype(jnp.int32)

    place = iota((n, toks), 0)
    block, row = lax.shift_right_logical(place, 4), place & (ROWS - 1)
    mine = block == ids
    pick_x = hot(mine & (row == rank))
    pick_d = hot(mine & (row == rank + CAP))
    piece = lax.shift_right_logical(row, 2)
    late = mine & ((row & 3) + SPARE == rank)
    pick_tail = [hot(late & (piece == c)) for c in range(4)]

    loads[0].wait()
    loads[1].wait()
    own_x = tq[...]
    own_d = (cq[...].astype(F32) * probs_col).astype(BF)
    main = dot(jnp.concatenate([pick_x, pick_d], 1), jnp.concatenate([own_x, own_d], 0))
    tail = dot(
        jnp.concatenate(pick_tail, 1),
        jnp.concatenate([own_d[:, LANES * c : LANES * (c + 1)] for c in range(4)], 0),
    )
    sb[:, :, 0:quarter] = main.astype(BF).reshape(nz, ROWS, quarter)
    sb[:, :, quarter : quarter + LANES] = tail.astype(BF).reshape(nz, ROWS, LANES)

    pl.semaphore_wait(barrier, len(peers))

    def hop(k):
        return hz + (1 - 2 * lax.rem(k, 2)) * lax.div(k + 1, 2)

    def z_send(k):
        d = hop(k)
        dst = lax.rem(z + d, nz)
        return remote(sb.at[dst], rb.at[t, z], zs.at[k], zr.at[k], ep_at(d))

    def z_source(k):
        return lax.rem(z - hop(k) + nz, nz)

    def z_recv(k):
        return remote(sb.at[0], rb.at[t, z_source(k)], zs.at[k], zr.at[k], ep_at(1))

    own_block = pltpu.make_async_copy(sb.at[z], rb.at[t, z], ld.at[5])
    own_block.start()

    def start_send(k, carry):
        z_send(k).start()
        return carry

    lax.fori_loop(0, nz - 1, start_send, 0)

    left_q, right_q, far_q = lax.rem(t + 3, 4), lax.rem(t + 1, 4), lax.rem(t + 2, 4)

    def pass_right(p, s):
        return remote(rb.at[t, s], rb.at[t, s], fs.at[0, p], fr.at[0, p], tp_at(1))

    def pass_left(p, s):
        return remote(rb.at[t, s], rb.at[t, s], fs.at[1, p], fr.at[1, p], tp_at(3))

    def from_left(p, s):
        return remote(rb.at[t, s], rb.at[left_q, s], fs.at[0, p], fr.at[0, p], tp_at(1))

    def from_right(p, s):
        return remote(rb.at[t, s], rb.at[right_q, s], fs.at[1, p], fr.at[1, p], tp_at(3))

    def onward(p, s, odd):
        q, to = (right_q, 3) if odd else (left_q, 1)
        return remote(rb.at[q, s], rb.at[q, s], fs.at[2, p], fr.at[2, p], tp_at(to))

    def from_far(p, s):
        return remote(rb.at[t, s], rb.at[far_q, s], fs.at[2, p], fr.at[2, p], tp_at(1))

    def share(p, s):
        pass_right(p, s).start()
        pass_left(p, s).start()

    def relay(p, s, odd):
        from_left(p, s).wait_recv()
        from_right(p, s).wait_recv()
        onward(p, s, odd).start()

    own_block.wait()
    share(0, z)
    z_recv(0).wait_recv()
    share(1, z_source(0))

    def gather(i, carry):
        for u in range(2):
            p = 2 * i + u
            z_recv(p - 1).wait_recv()
            share(p, z_source(p - 1))
        for u in range(2):
            p = 2 * i - 2 + u
            s = jnp.where(p == 0, z, z_source(jnp.maximum(p - 1, 0)))
            relay(p, s, u)
        return carry

    lax.fori_loop(1, hz, gather, 0)
    if nz > 2:
        relay(nz - 2, z_source(nz - 3), 0)
    else:
        relay(0, z, 0)
    relay(nz - 1, z_source(nz - 2), 1)
    from_far(0, z).wait_recv()

    def last(p, carry):
        from_far(p, z_source(p - 1)).wait_recv()
        return carry

    lax.fori_loop(1, nz, last, 0)

    rows = iota((m, n), 0)
    source = lax.shift_right_logical(rows * 6554, 16)
    slot = rows - CAP * source
    there = iota((m, n), 1)
    unpick_x = hot(there == ROWS * source + slot)
    unpick_d = hot((slot < SPARE) & (there == ROWS * source + CAP + slot))
    unpick_tail = [
        hot((slot >= SPARE) & (there == ROWS * source + 4 * c + slot - SPARE)) for c in range(4)
    ]
    unpick_main = jnp.concatenate([unpick_x, unpick_d], 0)
    unpick_tail = jnp.concatenate(unpick_tail, 0)
    per = quarter // band
    for q in range(4):
        got = rb[q].reshape(n, quarter + LANES)
        both = dot(unpick_main, got[:, 0:quarter])
        ends = dot(unpick_tail, got[:, quarter : quarter + LANES])
        ends = jnp.concatenate([ends[m * c : m * (c + 1)] for c in range(4)], 1)
        x_rows = both[0:m].astype(BF)
        d_rows = (both[m : 2 * m] + ends).astype(BF)
        for b in range(per):
            at = q * per + b
            xs[at // 2, at % 2] = x_rows[:, band * b : band * (b + 1)]
            ds[at // 2, at % 2] = d_rows[:, band * b : band * (b + 1)]

    mate_x = remote(xs.at[:, 1 - core], mx, ms.at[0], mr.at[0], mate)
    mate_d = remote(ds.at[:, 1 - core], md, ms.at[1], mr.at[1], mate)
    mate_g = remote(gt, mgt, ms.at[2], mr.at[2], mate)
    mate_x.start()
    mate_d.start()

    for copy in loads[2:]:
        copy.wait()
    gate_up = jnp.zeros((2 * ff, m), F32)
    back = jnp.zeros((ff, m), F32)
    for o in range(pairs):
        cols = pl.ds(2 * band * o, 2 * band)
        x_pair = jnp.concatenate([xs[o, 0], xs[o, 1]], 1)
        d_pair = jnp.concatenate([ds[o, 0], ds[o, 1]], 1)
        gate_up += dot(w[0 : 2 * ff, cols], x_pair, NT)
        back += dot(w[2 * ff : 3 * ff, cols], d_pair, NT)
    gate, up = gate_up[0:ff], gate_up[ff : 2 * ff]
    sigma = jax.nn.sigmoid(gate)
    active = gate * sigma
    hidden = (active * up).astype(BF)
    gt[0:ff, :] = (back * up * sigma * (1.0 + gate * (1.0 - sigma))).astype(BF)
    gt[ff : 2 * ff, :] = (back * active).astype(BF)
    gt[2 * ff : 3 * ff, :] = hidden
    mate_g.start()

    prob_row = jnp.sum(hidden.astype(F32) * back, 0, keepdims=True)
    in_source = iota((nz, m), 0) == lax.shift_right_logical(iota((nz, m), 1) * 6554, 16)
    at_row = iota((m, LANES), 0)
    at_slot = iota((m, LANES), 1) == at_row - CAP * lax.shift_right_logical(at_row * 6554, 16)
    pk[0] = dot(
        jnp.where(in_source, prob_row, 0.0), jnp.where(at_slot, 1.0, 0.0),
        precision=lax.Precision.HIGHEST,
    )
    prob_sends = [remote(pk.at[0], pk.at[r], ps.at[r], pr.at[r], tp_at(r)) for r in (1, 2, 3)]
    for copy in prob_sends:
        copy.start()

    eye_m = hot(iota((m, m), 0) == iota((m, m), 1))
    d_rows = dot(eye_m, gt[0 : 2 * ff, :], NT).astype(BF)

    def input_part(r):
        q = lax.rem(t + r, 4)
        cols = pl.ds(pl.multiple_of(q * quarter, quarter), quarter)
        ip[r] = dot(d_rows, w[0 : 2 * ff, cols]).astype(BF)

    low, high = pl.ds(0, half), pl.ds(half, half)
    to_right = [
        remote(ip.at[2, low], xa.at[0], hs.at[0, 0], hr.at[0, 0], tp_at(1)),
        remote(ip.at[1, high], xl.at[high], hs.at[0, 1], hr.at[0, 1], tp_at(1)),
        remote(ip.at[1, low], xl.at[low], hs.at[0, 2], hr.at[0, 2], tp_at(1)),
    ]
    to_left = [
        remote(ip.at[2, high], xa.at[1], hs.at[1, 0], hr.at[1, 0], tp_at(3)),
        remote(ip.at[3, low], xr.at[low], hs.at[1, 1], hr.at[1, 1], tp_at(3)),
        remote(ip.at[3, high], xr.at[high], hs.at[1, 2], hr.at[1, 2], tp_at(3)),
    ]
    input_part(2)
    to_right[0].start()
    to_left[0].start()

    def weight_part(j):
        o = lax.rem(y + j, ny)
        x_own, d_own, x_mate, d_mate = xs[o, core], ds[o, core], mx[o], md[o]
        ch[j, 0 : 2 * ff, :] = dot(gt[0 : 2 * ff, :], x_own) + dot(mgt[0 : 2 * ff, :], x_mate)
        ch[j, 2 * ff : 3 * ff, :] = dot(gt[2 * ff : 3 * ff, :], d_own) + dot(
            mgt[2 * ff : 3 * ff, :], d_mate
        )

    def y_copy(side, dist, part):
        j = dist if side == 0 else ny - dist
        where = part_b if part else part_a
        into = (yl, yr)[side]
        return remote(
            cs.at[j, where], into.at[dist - 1, where],
            ys.at[side, dist, part], yrs.at[side, dist, part], y_at(1 if side == 0 else ny - 1),
        )

    def y_step(side, dist, part):
        j = dist if side == 0 else ny - dist
        where = part_b if part else part_a
        alone = dist == hy or (dist == hy - 1 and part == 1 - side)
        if alone:
            cs[j, where, :] = ch[j, where, :].astype(BF)
        else:
            y_copy(side, dist + 1, part).wait_recv()
            came = (yl, yr)[side][dist, where, :].astype(F32)
            cs[j, where, :] = (ch[j, where, :] + came).astype(BF)
        y_copy(side, dist, part).start()

    mate_x.wait_recv()
    mate_d.wait_recv()
    mate_g.wait_recv()
    weight_part(hy)
    y_step(0, hy, 0)
    y_step(1, hy, 1)
    weight_part(hy - 1)
    y_step(0, hy - 1, 1)
    weight_part(ny - hy + 1)
    y_step(1, hy - 1, 0)

    input_part(1)
    to_right[1].start()
    input_part(3)
    to_left[1].start()
    for dist in range(hy - 2, 0, -1):
        weight_part(dist)
        weight_part(ny - dist)
    to_right[0].wait_recv()
    ip[1, low, :] = (ip[1, low, :].astype(F32) + xa[0].astype(F32)).astype(BF)
    to_right[2].start()
    to_left[0].wait_recv()
    ip[3, high, :] = (ip[3, high, :].astype(F32) + xa[1].astype(F32)).astype(BF)
    to_left[2].start()
    y_step(0, hy - 1, 0)
    y_step(1, hy - 1, 1)
    input_part(0)
    weight_part(0)
    if hy > 2:
        y_step(0, hy - 2, 1)
        y_step(1, hy - 2, 0)

    for copy in prob_sends:
        copy.wait_recv()
    prob = (pk[0] + pk[1]) + (pk[2] + pk[3])
    prob_high = prob.astype(BF)
    prob_low = (prob - prob_high.astype(F32)).astype(BF)
    to = iota((n, m), 0)
    block, row = lax.shift_right_logical(to, 4), to & (ROWS - 1)
    first = CAP * block
    frm = iota((n, m), 1)
    pack = hot((row < CAP) & (frm == first + row))
    pack_0 = hot((row >= CAP) & (frm == first + row - CAP))
    pack_1 = hot((row >= CAP) & (row < ROWS - 2) & (frm == first + row - CAP + SPARE))
    to = iota((n, nz), 0)
    block, row = lax.shift_right_logical(to, 4), to & (ROWS - 1)
    same = block == iota((n, nz), 1)
    pack_high, pack_low = hot(same & (row == CAP)), hot(same & (row == CAP + 1))
    to_right[1].wait_recv()
    to_left[1].wait_recv()
    to_right[2].wait_recv()
    to_left[2].wait_recv()
    summed = (
        ip[0].astype(F32) + (xl[...].astype(F32) + xr[...].astype(F32))
    ).astype(BF)
    ends = summed[:, 3 * LANES : 4 * LANES]
    packed = dot(pack, summed[:, 0 : 3 * LANES])
    packed = packed + jnp.concatenate(
        [dot(pack_0, ends), dot(pack_1, ends), dot(pack_high, prob_high) + dot(pack_low, prob_low)], 1
    )
    rs[...] = packed.astype(BF).reshape(nz, ROWS, 3 * LANES)

    def back_send(k):
        d = hop(k)
        dst = lax.rem(z + d, nz)
        return remote(rs.at[dst], rr.at[z], vs.at[k], vr.at[k], ep_at(d))

    def back_recv(k):
        return remote(rs.at[0], rr.at[z_source(k)], vs.at[k], vr.at[k], ep_at(1))

    def start_back(k, carry):
        back_send(k).start()
        return carry

    lax.fori_loop(0, nz - 1, start_back, 0)
    own_back = pltpu.make_async_copy(rs.at[z], rr.at[z], ld.at[6])
    own_back.start()

    for dist in range(hy - 2, 0, -1):
        if dist < hy - 2:
            y_step(0, dist, 1)
            y_step(1, dist, 0)
        y_step(0, dist, 0)
        y_step(1, dist, 1)
    for part in (0, 1):
        for side in (0, 1):
            y_copy(side, 1, 1 - part if side == 0 else part).wait_recv()
    total = ch[0] + (yl[0].astype(F32) + yr[0].astype(F32))
    gg_ref[...] = total[0:ff]
    gu_ref[...] = total[ff : 2 * ff]
    gd_ref[...] = total[2 * ff : 3 * ff]

    at = iota((toks, n), 1)
    block, row = lax.shift_right_logical(at, 4), at & (ROWS - 1)
    mine = block == ids_col
    take = hot(mine & (row == rank_col))
    take_0 = hot(mine & (row == rank_col + CAP) & (rank_col < SPARE))
    take_1 = hot(mine & (row == rank_col + CAP - SPARE) & (rank_col >= SPARE))
    take_high, take_low = hot(mine & (row == CAP)), hot(mine & (row == CAP + 1))

    def wait_back(k, carry):
        back_recv(k).wait_recv()
        return carry

    lax.fori_loop(0, nz - 1, wait_back, 0)
    own_back.wait()
    got = rr[...].reshape(n, 3 * LANES)
    tg_ref[:, 0 : 3 * LANES] = dot(take, got).astype(BF)
    tg_ref[:, 3 * LANES : 4 * LANES] = (
        dot(take_0, got[:, 0:LANES]) + dot(take_1, got[:, LANES : 2 * LANES])
    ).astype(BF)
    ends = got[:, 2 * LANES : 3 * LANES]
    chosen = iota((toks, LANES), 1) == rank_col
    value = jnp.where(chosen, dot(take_high, ends) + dot(take_low, ends), 0.0)
    value = jnp.sum(value, 1, keepdims=True) / probs_col
    pg_ref[...] = jnp.sum(jnp.where(eye, value, 0.0), 0, keepdims=True)

    def left_z(k, carry):
        z_send(k).wait_send()
        back_send(k).wait_send()
        return carry

    lax.fori_loop(0, nz - 1, left_z, 0)

    def left_x(i, carry):
        for u in range(2):
            p = 2 * i + u
            pass_right(p, z).wait_send()
            pass_left(p, z).wait_send()
            onward(p, z, u).wait_send()
        return carry

    lax.fori_loop(0, hz, left_x, 0)
    for copy in [mate_x, mate_d, mate_g] + prob_sends + to_right + to_left:
        copy.wait_send()
    for side in (0, 1):
        y_copy(side, hy, side).wait_send()
        for dist in range(hy - 1, 0, -1):
            for part in (0, 1):
                y_copy(side, dist, part).wait_send()


def shards(tokens, cotangent, expert_ids, gate_probs, w_gate, w_up, w_down):
    toks, width = tokens.shape
    ff = w_down.shape[1]
    nz, ny = lax.axis_size("ep"), lax.axis_size("island") // 2
    quarter, band = width // 4, width // (2 * ny)
    m = nz * CAP
    wide = quarter + LANES
    hy, hz = ny // 2, nz // 2
    hbm = pl.BlockSpec(memory_space=pl.ANY)
    vmem = pl.BlockSpec(memory_space=pltpu.VMEM)
    dma = pltpu.SemaphoreType.DMA
    token_grad, prob_grad, grad_gate, grad_up, grad_down = pl.pallas_call(
        functools.partial(kernel, nz, ny),
        out_shape=(
            jax.ShapeDtypeStruct((toks, quarter), BF),
            jax.ShapeDtypeStruct((1, toks), F32),
            jax.ShapeDtypeStruct((ff, band), F32),
            jax.ShapeDtypeStruct((ff, band), F32),
            jax.ShapeDtypeStruct((ff, band), F32),
        ),
        in_specs=[hbm, hbm, vmem, vmem, hbm, hbm, hbm],
        out_specs=(vmem,) * 5,
        scratch_shapes=[
            pltpu.VMEM((3 * ff, width), BF),
            pltpu.VMEM((toks, quarter), BF),
            pltpu.VMEM((toks, quarter), BF),
            pltpu.VMEM((nz, ROWS, wide), BF),
            pltpu.VMEM((4, nz, ROWS, wide), BF),
            pltpu.VMEM((ny, 2, m, band), BF),
            pltpu.VMEM((ny, 2, m, band), BF),
            pltpu.VMEM((ny, m, band), BF),
            pltpu.VMEM((ny, m, band), BF),
            pltpu.VMEM((3 * ff, m), BF),
            pltpu.VMEM((3 * ff, m), BF),
            pltpu.VMEM((ny, 3 * ff, band), F32),
            pltpu.VMEM((ny, 3 * ff, band), BF),
            pltpu.VMEM((hy, 3 * ff, band), BF),
            pltpu.VMEM((hy, 3 * ff, band), BF),
            pltpu.VMEM((4, m, quarter), BF),
            pltpu.VMEM((2, m // 2, quarter), BF),
            pltpu.VMEM((m, quarter), BF),
            pltpu.VMEM((m, quarter), BF),
            pltpu.VMEM((4, nz, LANES), F32),
            pltpu.VMEM((nz, ROWS, 3 * LANES), BF),
            pltpu.VMEM((nz, ROWS, 3 * LANES), BF),
            dma((7,)),
            dma((nz,)), dma((nz,)),
            dma((3, nz)), dma((3, nz)),
            dma((3,)), dma((3,)),
            dma((4,)), dma((4,)),
            dma((2, 3)), dma((2, 3)),
            dma((2, hy + 1, 2)), dma((2, hy + 1, 2)),
            dma((nz,)), dma((nz,)),
        ],
        compiler_params=pltpu.CompilerParams(
            collective_id=0, has_side_effects=True, vmem_limit_bytes=56 * 1024 * 1024
        ),
    )(
        tokens, cotangent,
        expert_ids.reshape(1, toks), gate_probs.reshape(1, toks),
        w_gate[0].T, w_up[0].T, w_down[0],
    )
    return (
        token_grad, prob_grad.reshape(toks, 1),
        grad_gate.T[None], grad_up.T[None], grad_down[None],
    )


def solution(mesh):
    rows = P(("island", "ep"), None)
    in_specs = (rows, rows, rows, rows, P("ep", None, "tp"), P("ep", None, "tp"), P("ep", "tp", None))
    out_specs = (
        P(("island", "ep"), "tp"), rows,
        P("ep", "island", "tp"), P("ep", "island", "tp"), P("ep", "tp", "island"),
    )
    return jax.shard_map(shards, mesh=mesh, in_specs=in_specs, out_specs=out_specs, check_vma=False)
```

time: 405 us -> 85 us (0.21)
  waiting for transfers between devices: 271 us -> 0 us
  Pallas kernels: 0 us -> 79.5 us
  starting transfers between devices: 55.1 us -> 0 us
  local copies, waits for them, and re-layouts: 36.8 us -> 4.62 us
  between operations: 14.1 us -> 0.66 us
  matrix products: 10.9 us -> 0 us
  blocking collectives: 9.36 us -> 0 us
  other arithmetic: 6.12 us -> 0 us
    unnamed x7 -> x0, waiting for transfers between devices: 172 us -> none
    all_to_all x5 -> x0, waiting for transfers between devices: 98.7 us -> none  [the longest x1 42.8 us: shards(): lax.all_to_all(send_dy, 'ep', split_axis=0, concat_axis=1, tiled=True)]
    pallas_call x0 -> x1, Pallas kernels: none -> 79.5 us  [shards(): pl.pallas_call(functools.partial(kernel, nz, ny), out_shape=(jax.ShapeDty...]
    all_to_all x5 -> x0, starting transfers between devices: 54.9 us -> none  [the longest x1 19.4 us: shards(): lax.all_to_all(send_p.astype(jnp.bfloat16), 'ep', split_axis=0, concat_ax...]
    unnamed x26 -> x13, local copies, waits for them, and re-layouts: 22.6 us -> 4.62 us
    dot_general x8 -> x0, matrix products: 10.9 us -> none  [the longest x1 2.23 us: shards(): jnp.einsum('emd,emf->edf', recv_x, d_gate, preferred_element_type=jnp.flo...]
    psum x1 -> x0, blocking collectives: 9.36 us -> none  [shards(): prob_rows = lax.psum(prob_part, 'tp')]
    gather x4 -> x0, local copies, waits for them, and re-layouts: 5.35 us -> none  [the longest x1 1.77 us: shards(): prob_grad = back_probs.reshape(-1)[dest].reshape(tok_rows, top_count)]
  transfers between devices with their start and end apart: 9 -> 0, of which waited for: 7 -> 0; matrix products, arithmetic and copies ran while one was open for 11% -> 0% of each run, Pallas kernels for 0% -> 0%
where the time goes in v1:
time: 85 us; the launch traced here: 84.7 us
  Pallas kernels  79.5 us (94%)
  local copies, waits for them, and re-layouts  4.62 us (5%)
    pallas_call x1, Pallas kernels, shards(): pl.pallas_call(functools.partial(kernel, nz, ny), out_shape=(jax.ShapeDty...  79.5 us
    unnamed x13, local copies, waits for them, and re-layouts  4.62 us

profile of v1, /device:TPU:1, one launch (start us, length us, event | category | flops | bytes accessed | tf_op | source)
XLA Modules:
  0.0 84.7 jit_solution(772352622070769301)
XLA Ops:
  0.6 79.5 %shard_map.110 = (bf16[128,512]{1,0:T(8,128)(2,1)}, f32[1,128]{1,0:T(1,128)}, f32[192,128]{1,0:T(8,128)}, f32[192,128]{1,0:T(8,128)}, f32[192,128]{1,0:T(8,128)}) custom-call(bf16[128,2048]{1,0:T(8,128)(2,1)} %tok.1, bf16[128,2048]{1,0:T(8,128)(2,1)} %cot.1, s32[1,128]{1,0:T(1,128)} %bitcast.23, f32[1,128]{1,0:T(1,128)} %bitcast.24, ...), custom_call_target="tpu_custom_call" | custom-call | tf_op jit(solution)/shard_map/pallas_call | solution.py:476
  80.1 0.0 copy-start.3
  80.1 0.0 copy-start.2
  80.1 1.6 %copy.17 = bf16[128,512]{1,0:T(8,128)(2,1)} copy(bf16[128,512]{1,0:T(8,128)(2,1)} %get-tuple-element.20) | data formatting | bytes 262144
  81.7 0.0 copy-done.3
  81.7 0.5 copy.18
  82.2 0.0 copy-done.2
  82.2 0.0 copy-start.1
  82.2 0.6 copy.19
  82.9 0.3 copy-done.1
  83.2 0.0 copy-start
  83.2 0.6 copy.20
  83.8 0.3 copy-done
  84.1 0.6 copy.21
Async XLA Ops:
  80.1 1.6 %copy-start.3 = (f32[1,128]{1,0:T(1,128)S(1)}, f32[1,128]{1,0:T(1,128)}, u32[]{:S(2)}) copy-start(f32[1,128]{1,0:T(1,128)} %get-tuple-element.11) | copy-start | bytes 1540
  80.1 2.1 %copy-start.2 = (f32[192,128]{1,0:T(8,128)S(1)}, f32[192,128]{1,0:T(8,128)}, u32[]{:S(2)}) copy-start(f32[192,128]{1,0:T(8,128)} %get-tuple-element.12) | copy-start | bytes 294916
  82.2 0.9 %copy-start.1 = (f32[192,128]{1,0:T(8,128)S(1)}, f32[192,128]{1,0:T(8,128)}, u32[]{:S(2)}) copy-start(f32[192,128]{1,0:T(8,128)} %get-tuple-element.13) | copy-start | bytes 294916
  83.2 0.9 %copy-start = (f32[192,128]{1,0:T(8,128)S(1)}, f32[192,128]{1,0:T(8,128)}, u32[]{:S(2)}) copy-start(f32[192,128]{1,0:T(8,128)} %get-tuple-element.14) | copy-start | bytes 294916
